TPU v7x, 32 devices: a whole 2x2x4 slice. The times are simulated.
32 devices in a mesh: row: 4 (over y, core), col: 8 (over z, x).
Axes of the slice: x: 2, y: 2, z: 4, core: 2. Of those that a mesh axis runs over, the one named last changes fastest.
Arguments:
- transition: bfloat16 [32768, 32768], P('row', 'col'), may hold values from 1.5258789e-06 to 0.0024414062, as said below
- emission: bfloat16 [96, 32768], P(None, 'col'), may hold values from 0.0099487305 to 1
- token_ids: int32 [2, 192], replicated, may hold values from 0 to 95
- forward: bfloat16 [2, 192, 32768], P(None, 'col', 'row'), may hold values from 3.0517578e-06 to 0.0008239746, as said below
- backward_last: float32 [192, 32768], P('row', 'col'), may hold values from 0.1 to 10
Outputs:
- backward: float32 [2, 192, 32768], P(None, 'col', 'row')
- counts: float32 [32768, 1024], P('row', 'col')
Inputs may be any that keep to these rules, and one draw needn't show every extreme that they name: Positive transition weights. Positive forward weights.
All inputs are finite; a program needn't handle non-finite values.
Results may differ from a plain program's by a relative error of at most 0.00048.
Values may be sent and summed in bfloat16 or wider, within the bound.
A program may use at most 192 MiB of HBM per device.

v0:
```python
import jax
import jax.numpy as jnp
from jax import lax
from jax.sharding import PartitionSpec as P

H = 32768
N = 192
DW = 128


def spread(value, axis, source):
    kept = jnp.where(lax.axis_index(axis) == source, value, 0).astype(value.dtype)
    return lax.psum(kept, axis)


def on_device(transition, emission, token_ids, forward, backward_last):
    row_count = lax.axis_size("row")
    col_count = lax.axis_size("col")
    col_index = lax.axis_index("col")
    ratio = col_count // row_count
    local_seqs = forward.shape[1]
    block_src = transition.shape[0]
    block_dst = transition.shape[1]
    seq_total = local_seqs * col_count
    forward_all = lax.all_gather(forward, "col", axis=1, tiled=True)
    backward_next = lax.all_gather(backward_last, "row", axis=0, tiled=True)
    columns = lax.broadcasted_iota(jnp.int32, (seq_total, emission.shape[0]), 1)
    window = transition[:, :DW]
    totals = jnp.zeros((block_src, DW), jnp.float32)
    outputs = [None, None]
    for step in (1, 0):
        onehot = (token_ids[step][:, None] == columns).astype(jnp.bfloat16)
        emitted = jnp.dot(onehot, emission, preferred_element_type=jnp.float32)
        weighted_back = (emitted * backward_next).astype(jnp.bfloat16)
        partial_value = lax.dot_general(
            weighted_back, transition, (((1,), (1,)), ((), ())), preferred_element_type=jnp.float32
        )
        alpha_all = forward_all[step].astype(jnp.float32)
        summed = lax.psum(partial_value, "col")
        mine = lax.dynamic_slice_in_dim(summed, col_index * local_seqs, local_seqs, 0)
        alpha_mine = forward[step].astype(jnp.float32)
        local_norm = lax.psum(jnp.sum(alpha_mine * mine, axis=1), "row")
        normal_all = lax.all_gather(local_norm, "col", axis=0, tiled=True)
        normal_mine = lax.dynamic_slice_in_dim(normal_all, col_index * local_seqs, local_seqs, 0)
        outputs[step] = mine / normal_mine[:, None]
        scaled = (alpha_all / normal_all[:, None]).astype(jnp.bfloat16)
        totals = totals + lax.dot_general(
            scaled,
            weighted_back[:, :DW],
            (((0,), (0,)), ((), ())),
            preferred_element_type=jnp.float32,
        )
        if step == 1:
            whole = summed / normal_all[:, None]
            piece = lax.dynamic_slice_in_dim(whole, col_index % ratio * block_dst, block_dst, 1)
            backward_next = spread(piece, "row", col_index // ratio)
    counts = window.astype(jnp.float32) * totals * (H * H / N)
    return (jnp.stack(outputs), counts)


def solution(mesh):
    in_specs = (P("row", "col"), P(None, "col"), P(), P(None, "col", "row"), P("row", "col"))
    out_specs = (P(None, "col", "row"), P("row", "col"))
    return jax.shard_map(
        on_device, mesh=mesh, in_specs=in_specs, out_specs=out_specs, check_vma=False
    )
```

profile of v0, /device:TPU:0, one launch (start us, length us, event | category | flops | bytes accessed | tf_op | source)
XLA Modules:
  0.0 741.6 jit_solution(9007567216397277755)
XLA Ops:
  7.2 0.7 all-gather.3.cloned.1.call-update
  8.0 0.8 fusion.17
  8.7 32.1 %all-gather.3.cloned.1.call-done = f32[192,4096]{1,0:T(8,128)} async-done(((f32[48,4096]{1,0:T(8,128)}), f32[192,4096]{1,0:T(8,128)}) %all-gather.3.cloned.1.call-update) | async-done | bytes 3145744 | tf_op jit(solution)/shard_map/all_gather | solution.py:26
  40.8 2.5 fusion.5
  43.3 31.1 %fusion.18 = f32[192,8192]{1,0:T(8,128)} fusion(bf16[192,4096]{1,0:T(8,128)(2,1)S(1)} %fusion.5, bf16[8192,4096]{1,0:T(8,128)(2,1)} %param.5), kind=kOutput, calls=%fused_computation.31 | convolution fusion | flops 12884901888 | bytes 74973184 | tf_op jit(solution)/shard_map/dot_general | solution.py:35
  75.1 0.6 dynamic-slice
  76.4 209.8 %all-reduce.6.cloned.1.call-done = f32[192,8192]{1,0:T(8,128)} async-done(((f32[192,8192]{1,0:T(8,128)}), f32[192,8192]{1,0:T(8,128)}) %all-reduce.6.cloned.1.call-update) | async-done | bytes 6291472 | tf_op jit(solution)/shard_map/psum | solution.py:39
  286.2 1.3 fusion.12
  287.5 6.9 psum.36
  294.7 19.4 %all-reduce = f32[192]{0:T(256)S(1)} all-reduce(f32[192]{0:T(256)S(1)} %dynamic-update-slice), channel_id=1, replica_groups=mesh['row'=4,'col'=8] {'col'}, use_global_device_ids=true, to_apply=%add | all-reduce | flops 192 | bytes 1536
  314.1 4.0 fusion.7
  318.7 64.3 %all-reduce.8.cloned.1.call-done = f32[192,4096]{1,0:T(8,128)} async-done(((f32[192,4096]{1,0:T(8,128)}), f32[192,4096]{1,0:T(8,128)}) %all-reduce.8.cloned.1.call-update) | async-done | bytes 3145744 | tf_op jit(solution)/shard_map/psum | solution.py:13
  383.0 3.7 fusion.4
  386.7 30.8 %fusion.19 = f32[192,8192]{1,0:T(8,128)} fusion(bf16[192,4096]{1,0:T(8,128)(2,1)} %fusion.4, bf16[8192,4096]{1,0:T(8,128)(2,1)} %param.5), kind=kOutput, calls=%fused_computation.32 | convolution fusion | flops 12884901888 | bytes 74973184 | tf_op jit(solution)/shard_map/dot_general | solution.py:35
  417.6 66.8 %all-gather.5.cloned.1.call-done = bf16[2,192,8192]{2,1,0:T(8,128)(2,1)} async-done(((bf16[2,24,8192]{2,1,0:T(8,128)(2,1)}), bf16[2,192,8192]{2,1,0:T(8,128)(2,1)}) %all-gather.5.cloned.1.call-update) | async-done | bytes 6291472 | tf_op jit(solution)/shard_map/all_gather | solution.py:25
  484.4 5.4 fusion.9
  489.9 1.3 divide_bitcast_fusion
  491.1 207.2 %all-reduce.10.cloned.1.call-done = f32[192,8192]{1,0:T(8,128)} async-done(((f32[192,8192]{1,0:T(8,128)}), f32[192,8192]{1,0:T(8,128)}) %all-reduce.10.cloned.1.call-update) | async-done | bytes 6291472 | tf_op jit(solution)/shard_map/psum | solution.py:39
  698.3 1.3 fusion.11
  699.6 6.9 psum.39
  706.7 19.4 %all-reduce.1 = f32[192]{0:T(256)S(1)} all-reduce(f32[192]{0:T(256)S(1)} %dynamic-update-slice.1), channel_id=1, replica_groups=mesh['row'=4,'col'=8] {'col'}, use_global_device_ids=true, to_apply=%add.1 | all-reduce | flops 192 | bytes 1536
  726.2 1.4 divide_bitcast_fusion.1
  727.6 1.2 pad_maximum_fusion
  728.9 6.2 fusion.1
  (25 shorter events, 2.0 us)
Async XLA Ops:
  7.2 33.7 %copy-start = (bf16[96,4096]{1,0:T(8,128)(2,1)S(1)}, bf16[96,4096]{1,0:T(8,128)(2,1)}, u32[]{:S(2)}) copy-start(bf16[96,4096]{1,0:T(8,128)(2,1)} %param.6) | copy-start | bytes 2359300
  7.2 33.7 %all-gather.3.cloned.1.call-start = ((), (), s32[]{:S(2)}) async-start(), calls=%async_computation | async-start | bytes 3932160 | tf_op jit(solution)/shard_map/all_gather | solution.py:26
  7.9 278.3 %all-reduce.6.cloned.1.call-start = ((), (), s32[]{:S(2)}) async-start(), calls=%async_computation.1 | async-start | bytes 12582912 | tf_op jit(solution)/shard_map/psum | solution.py:39
  74.5 0.7 copy-start.3
  74.5 211.8 %copy-start.1 = (bf16[2,24,8192]{2,1,0:T(8,128)(2,1)S(1)}, bf16[2,24,8192]{2,1,0:T(8,128)(2,1)}, u32[]{:S(2)}) copy-start(bf16[2,24,8192]{2,1,0:T(8,128)(2,1)} %param.8) | copy-start | bytes 2359300
  74.5 308.5 %all-reduce.8.cloned.1.call-start = ((), (), s32[]{:S(2)}) async-start(), calls=%async_computation.2 | async-start | bytes 6291456 | tf_op jit(solution)/shard_map/psum | solution.py:13
  318.1 166.4 %all-gather.5.cloned.1.call-start = ((), (), s32[]{:S(2)}) async-start(), calls=%async_computation.4 | async-start | bytes 7077888 | tf_op jit(solution)/shard_map/all_gather | solution.py:25
  318.7 379.7 %all-reduce.10.cloned.1.call-start = ((), (), s32[]{:S(2)}) async-start(), calls=%async_computation.3 | async-start | bytes 12582912 | tf_op jit(solution)/shard_map/psum | solution.py:39
  417.6 280.7 %copy-start.2 = (bf16[2,24,8192]{2,1,0:T(8,128)(2,1)S(1)}, bf16[2,24,8192]{2,1,0:T(8,128)(2,1)}, u32[]{:S(2)}) copy-start(bf16[2,24,8192]{2,1,0:T(8,128)(2,1)} %param.8) | copy-start | bytes 2359300
  726.1 2.7 copy-start.4
Sparse Core Ops, SparseCore 0:
  9.6 31.2 all-gather.2
  74.6 211.5 all-reduce.5
  318.2 64.7 all-reduce.7
  385.3 99.1 all-gather.4
  488.5 209.7 all-reduce.9
where the time goes:
time: 742 us
  waiting for transfers between devices  582 us (78%)
  matrix products  79.7 us (11%)
  blocking collectives  52.5 us (7%)
  between operations  14.5 us (2%)
  other arithmetic  10.5 us (1%)
    psum x2, waiting for transfers between devices, on_device(): summed = lax.psum(partial_value, 'col')  417 us
    all_gather x1, waiting for transfers between devices, on_device(): forward_all = lax.all_gather(forward, 'col', axis=1, tiled=True)  66.8 us
    psum x1, waiting for transfers between devices, spread(): return lax.psum(kept, axis)  64.3 us
    dot_general x2, matrix products, on_device(): lax.dot_general(weighted_back, transition, (((1,), (1,)), ((), ())), pref...  61.9 us
    unnamed x2, blocking collectives  38.8 us
    all_gather x1, waiting for transfers between devices, on_device(): backward_next = lax.all_gather(backward_last, 'row', axis=0, tiled=True)  32.1 us
  transfers between devices with their start and end apart: 5, of which 5 were waited for; matrix products, arithmetic and copies ran while one was open for 6% of the time, Pallas kernels for 0%

commit v1 on v0

--- a/solution.py
+++ b/solution.py
@@ -6,6 +6,17 @@
 H = 32768
 N = 192
 DW = 128
+
+
+def gather_by_hops(x, mesh_axis, along):
+    count = lax.axis_size(mesh_axis)
+    right = [(i, (i + 1) % count) for i in range(count)]
+    parts = [x]
+    for far in range(1, count):
+        parts = [lax.ppermute(parts[0], mesh_axis, right), *parts]
+    whole = jnp.concatenate(parts, axis=along)
+    shift = (lax.axis_index(mesh_axis) + 1) * parts[-1].shape[along]
+    return jnp.roll(whole, shift, axis=along)
 
 
 def spread(value, axis, source):
@@ -22,7 +33,7 @@
     block_src = transition.shape[0]
     block_dst = transition.shape[1]
     seq_total = local_seqs * col_count
-    forward_all = lax.all_gather(forward, "col", axis=1, tiled=True)
+    forward_all = gather_by_hops(forward, "col", 1)
     backward_next = lax.all_gather(backward_last, "row", axis=0, tiled=True)
     columns = lax.broadcasted_iota(jnp.int32, (seq_total, emission.shape[0]), 1)
     window = transition[:, :DW]

time: 742 us -> 766 us (1.032)
  local copies, waits for them, and re-layouts: 2.54 us -> 29.1 us
  waiting for transfers between devices: 582 us -> 573 us
    ppermute x0 -> x7, waiting for transfers between devices: none -> 116 us  [gather_by_hops(): parts = [lax.ppermute(parts[0], mesh_axis, right), *parts]]
    all_gather x1 -> x0, waiting for transfers between devices: 66.8 us -> none  [on_device(): forward_all = lax.all_gather(forward, 'col', axis=1, tiled=True)]
    all_gather x1, waiting for transfers between devices: 32.1 us -> 0.01 us  [on_device(): backward_next = lax.all_gather(backward_last, 'row', axis=0, tiled=True)]
    unnamed x15 -> x36, local copies, waits for them, and re-layouts: 1.62 us -> 27.2 us
    psum x2, waiting for transfers between devices: 417 us -> 396 us  [on_device(): summed = lax.psum(partial_value, 'col')]
  transfers between devices with their start and end apart: 5 -> 11, of which waited for: 5 -> 9; matrix products, arithmetic and copies ran while one was open for 6% -> 9% of each run, Pallas kernels for 0% -> 0%
where the time goes in v1:
time: 766 us; the launch traced here: 765 us
  waiting for transfers between devices  573 us (75%)
  matrix products  81.9 us (11%)
  blocking collectives  52.5 us (7%)
  local copies, waits for them, and re-layouts  29.1 us (4%)
  between operations  14.5 us (2%)
  other arithmetic  10.4 us (1%)
    psum x2, waiting for transfers between devices, on_device(): summed = lax.psum(partial_value, 'col')  396 us
    ppermute x7, waiting for transfers between devices, gather_by_hops(): parts = [lax.ppermute(parts[0], mesh_axis, right), *parts]  116 us
    dot_general x2, matrix products, on_device(): lax.dot_general(weighted_back, transition, (((1,), (1,)), ((), ())), pref...  61.3 us
    psum x1, waiting for transfers between devices, spread(): return lax.psum(kept, axis)  60.5 us
    unnamed x2, blocking collectives  38.8 us
    unnamed x36, local copies, waits for them, and re-layouts  27.2 us
  transfers between devices with their start and end apart: 11, of which 9 were waited for; matrix products, arithmetic and copies ran while one was open for 9% of the time, Pallas kernels for 0%

profile of v1, /device:TPU:0, one launch (start us, length us, event | category | flops | bytes accessed | tf_op | source)
XLA Modules:
  0.0 764.5 jit_solution(13061276671822395665)
XLA Ops:
  7.2 3.0 collective-permute-start
  10.3 20.7 %collective-permute-done = bf16[2,24,8192]{2,1,0:T(8,128)(2,1)S(1)} collective-permute-done((bf16[2,24,8192]{2,1,0:T(8,128)(2,1)}, bf16[2,24,8192]{2,1,0:T(8,128)(2,1)S(1)}, u32[]{:S(2)}, u32[]{:S(2)}) %collective-permute-start) | collective-permute-done | bytes 786464 | tf_op jit(solution)/shard_map/ppermute | solution.py:16
  31.0 21.4 %collective-permute-done.1 = bf16[2,24,8192]{2,1,0:T(8,128)(2,1)S(1)} collective-permute-done((bf16[2,24,8192]{2,1,0:T(8,128)(2,1)S(1)}, bf16[2,24,8192]{2,1,0:T(8,128)(2,1)S(1)}, u32[]{:S(2)}, u32[]{:S(2)}) %collective-permute-start.1) | collective-permute-done | bytes 786464 | tf_op jit(solution)/shard_map/ppermute | solution.py:16
  52.4 20.5 %collective-permute-done.2 = bf16[2,24,8192]{2,1,0:T(8,128)(2,1)S(1)} collective-permute-done((bf16[2,24,8192]{2,1,0:T(8,128)(2,1)S(1)}, bf16[2,24,8192]{2,1,0:T(8,128)(2,1)S(1)}, u32[]{:S(2)}, u32[]{:S(2)}) %collective-permute-start.2) | collective-permute-done | bytes 786464 | tf_op jit(solution)/shard_map/ppermute | solution.py:16
  73.8 19.6 %collective-permute-done.3 = bf16[2,24,8192]{2,1,0:T(8,128)(2,1)S(1)} collective-permute-done((bf16[2,24,8192]{2,1,0:T(8,128)(2,1)S(1)}, bf16[2,24,8192]{2,1,0:T(8,128)(2,1)S(1)}, u32[]{:S(2)}, u32[]{:S(2)}) %collective-permute-start.3) | collective-permute-done | bytes 786464 | tf_op jit(solution)/shard_map/ppermute | solution.py:16
  94.3 18.7 %collective-permute-done.4 = bf16[2,24,8192]{2,1,0:T(8,128)(2,1)S(1)} collective-permute-done((bf16[2,24,8192]{2,1,0:T(8,128)(2,1)S(1)}, bf16[2,24,8192]{2,1,0:T(8,128)(2,1)S(1)}, u32[]{:S(2)}, u32[]{:S(2)}) %collective-permute-start.4) | collective-permute-done | bytes 786464 | tf_op jit(solution)/shard_map/ppermute | solution.py:16
  115.7 15.1 %collective-permute-done.5 = bf16[2,24,8192]{2,1,0:T(8,128)(2,1)} collective-permute-done((bf16[2,24,8192]{2,1,0:T(8,128)(2,1)S(1)}, bf16[2,24,8192]{2,1,0:T(8,128)(2,1)}, u32[]{:S(2)}, u32[]{:S(2)}) %collective-permute-start.5) | collective-permute-done | bytes 786464 | tf_op jit(solution)/shard_map/ppermute | solution.py:16
  130.8 3.6 fusion.5
  134.5 30.7 %fusion.20 = f32[192,8192]{1,0:T(8,128)} fusion(bf16[192,4096]{1,0:T(8,128)(2,1)} %fusion.5, bf16[8192,4096]{1,0:T(8,128)(2,1)} %param.5), kind=kOutput, calls=%fused_computation.49 | convolution fusion | flops 12884901888 | bytes 74973184 | tf_op jit(solution)/shard_map/dot_general | solution.py:46
  165.2 2.2 constant_dynamic-update-slice_fusion.15
  177.6 2.1 constant_dynamic-update-slice_fusion.7
  179.7 197.4 %all-reduce.6.cloned.1.call-done = f32[192,8192]{1,0:T(8,128)} async-done(((f32[192,8192]{1,0:T(8,128)}), f32[192,8192]{1,0:T(8,128)}) %all-reduce.6.cloned.1.call-update) | async-done | bytes 6291472 | tf_op jit(solution)/shard_map/psum | solution.py:50
  378.4 6.9 psum.36
  385.5 19.4 %all-reduce = f32[192]{0:T(256)S(1)} all-reduce(f32[192]{0:T(256)S(1)} %dynamic-update-slice), channel_id=1, replica_groups=mesh['row'=4,'col'=8] {'col'}, use_global_device_ids=true, to_apply=%add | all-reduce | flops 192 | bytes 1536
  404.9 4.0 fusion.7
  413.3 60.5 %all-reduce.8.cloned.1.call-done = f32[192,4096]{1,0:T(8,128)} async-done(((f32[192,4096]{1,0:T(8,128)}), f32[192,4096]{1,0:T(8,128)}) %all-reduce.8.cloned.1.call-update) | async-done | bytes 3145744 | tf_op jit(solution)/shard_map/psum | solution.py:24
  473.8 3.7 fusion.4
  477.5 30.7 %fusion.21 = f32[192,8192]{1,0:T(8,128)} fusion(bf16[192,4096]{1,0:T(8,128)(2,1)} %fusion.4, bf16[8192,4096]{1,0:T(8,128)(2,1)} %param.5), kind=kOutput, calls=%fused_computation.50 | convolution fusion | flops 12884901888 | bytes 74973184 | tf_op jit(solution)/shard_map/dot_general | solution.py:46
  508.2 2.2 constant_dynamic-update-slice_fusion.4
  514.3 5.4 fusion.9
  521.0 198.8 %all-reduce.10.cloned.1.call-done = f32[192,8192]{1,0:T(8,128)} async-done(((f32[192,8192]{1,0:T(8,128)}), f32[192,8192]{1,0:T(8,128)}) %all-reduce.10.cloned.1.call-update) | async-done | bytes 6291472 | tf_op jit(solution)/shard_map/psum | solution.py:50
  721.1 6.9 psum.39
  728.2 19.4 %all-reduce.1 = f32[192]{0:T(256)S(1)} all-reduce(f32[192]{0:T(256)S(1)} %dynamic-update-slice.1), channel_id=1, replica_groups=mesh['row'=4,'col'=8] {'col'}, use_global_device_ids=true, to_apply=%add.1 | all-reduce | flops 192 | bytes 1536
  747.7 7.8 %fusion.1 = f32[8192,128]{1,0:T(8,128)} fusion(f32[8192,128]{1,0:T(8,128)} %fusion.9, bf16[2,384,8192]{2,1,0:T(8,128)(2,1)} %constant_dynamic-update-slice_fusion, s32[]{:T(128)S(6)} %select_n.47, f32[192]{0:T(256)S(1)} %all-reduce.1, bf16[8192,4096]{1,0:T(8,128)(2,1)} %param.5, bf16[192,4096]{1,0:T(8,128)(2,1)} %fusion.4), kind=kOutput, calls=%fused_computation.2 | convolution fusion | flops 411566080 | bytes 13681412 | tf_op jit(solution)/shard_map/dot_general | solution.py:58
  (58 shorter events, 29.4 us)
Async XLA Ops:
  7.2 123.7 %copy-start = (bf16[96,4096]{1,0:T(8,128)(2,1)S(1)}, bf16[96,4096]{1,0:T(8,128)(2,1)}, u32[]{:S(2)}) copy-start(bf16[96,4096]{1,0:T(8,128)(2,1)} %param.6) | copy-start | bytes 2359300
  7.2 123.6 %all-gather.2.cloned.1.call-start = ((), (), s32[]{:S(2)}) async-start(), calls=%async_computation | async-start | bytes 3932160 | tf_op jit(solution)/shard_map/all_gather | solution.py:37
  7.2 23.8 %collective-permute-start = (bf16[2,24,8192]{2,1,0:T(8,128)(2,1)}, bf16[2,24,8192]{2,1,0:T(8,128)(2,1)S(1)}, u32[]{:S(2)}, u32[]{:S(2)}) collective-permute-start(bf16[2,24,8192]{2,1,0:T(8,128)(2,1)} %param.8), channel_id=1, source_target_pairs={{0,1},{1,2},{2,3},{3,4},{4,5},{5,6},{6,7},{7,0},{8,9},{9,10},{10,1... | collective-permute-start | bytes 2359304 | tf_op jit(solution)/shard_map/ppermute | solution.py:16
  10.2 366.8 %all-reduce.6.cloned.1.call-start = ((), (), s32[]{:S(2)}) async-start(), calls=%async_computation.1 | async-start | bytes 12582912 | tf_op jit(solution)/shard_map/psum | solution.py:50
  31.0 21.4 %collective-permute-start.1 = (bf16[2,24,8192]{2,1,0:T(8,128)(2,1)S(1)}, bf16[2,24,8192]{2,1,0:T(8,128)(2,1)S(1)}, u32[]{:S(2)}, u32[]{:S(2)}) collective-permute-start(bf16[2,24,8192]{2,1,0:T(8,128)(2,1)S(1)} %collective-permute-done), channel_id=1, source_target_pairs={{0,1},{1,2},{2,3},{3,4},{4,5},{5,6},{6,7},{7,0},{8,9},{9,10},{10,1... | collective-permute-start | bytes 2359304 | tf_op jit(solution)/shard_map/ppermute | solution.py:16
  52.4 20.5 %collective-permute-start.2 = (bf16[2,24,8192]{2,1,0:T(8,128)(2,1)S(1)}, bf16[2,24,8192]{2,1,0:T(8,128)(2,1)S(1)}, u32[]{:S(2)}, u32[]{:S(2)}) collective-permute-start(bf16[2,24,8192]{2,1,0:T(8,128)(2,1)S(1)} %collective-permute-done.1), channel_id=1, source_target_pairs={{0,1},{1,2},{2,3},{3,4},{4,5},{5,6},{6,7},{7,0},{8,9},{9,10},{10,1... | collective-permute-start | bytes 2359304 | tf_op jit(solution)/shard_map/ppermute | solution.py:16
  72.9 0.9 copy-start.3
  73.8 19.6 %collective-permute-start.3 = (bf16[2,24,8192]{2,1,0:T(8,128)(2,1)S(1)}, bf16[2,24,8192]{2,1,0:T(8,128)(2,1)S(1)}, u32[]{:S(2)}, u32[]{:S(2)}) collective-permute-start(bf16[2,24,8192]{2,1,0:T(8,128)(2,1)S(1)} %collective-permute-done.2), channel_id=1, source_target_pairs={{0,1},{1,2},{2,3},{3,4},{4,5},{5,6},{6,7},{7,0},{8,9},{9,10},{10,1... | collective-permute-start | bytes 2359304 | tf_op jit(solution)/shard_map/ppermute | solution.py:16
  93.4 0.9 copy-start.6
  94.3 18.7 %collective-permute-start.4 = (bf16[2,24,8192]{2,1,0:T(8,128)(2,1)S(1)}, bf16[2,24,8192]{2,1,0:T(8,128)(2,1)S(1)}, u32[]{:S(2)}, u32[]{:S(2)}) collective-permute-start(bf16[2,24,8192]{2,1,0:T(8,128)(2,1)S(1)} %collective-permute-done.3), channel_id=1, source_target_pairs={{0,1},{1,2},{2,3},{3,4},{4,5},{5,6},{6,7},{7,0},{8,9},{9,10},{10,1... | collective-permute-start | bytes 2359304 | tf_op jit(solution)/shard_map/ppermute | solution.py:16
  113.0 52.2 %copy-start.7 = (bf16[2,24,8192]{2,1,0:T(8,128)(2,1)}, bf16[2,24,8192]{2,1,0:T(8,128)(2,1)S(1)}, u32[]{:S(2)}) copy-start(bf16[2,24,8192]{2,1,0:T(8,128)(2,1)S(1)} %collective-permute-done.4) | copy-start | bytes 2359300
  113.0 17.8 %collective-permute-start.5 = (bf16[2,24,8192]{2,1,0:T(8,128)(2,1)S(1)}, bf16[2,24,8192]{2,1,0:T(8,128)(2,1)}, u32[]{:S(2)}, u32[]{:S(2)}) collective-permute-start(bf16[2,24,8192]{2,1,0:T(8,128)(2,1)S(1)} %collective-permute-done.4), channel_id=1, source_target_pairs={{0,1},{1,2},{2,3},{3,4},{4,5},{5,6},{6,7},{7,0},{8,9},{9,10},{10,1... | collective-permute-start | bytes 2359304 | tf_op jit(solution)/shard_map/ppermute | solution.py:16
  130.8 34.4 %collective-permute-start.6 = (bf16[2,24,8192]{2,1,0:T(8,128)(2,1)}, bf16[2,24,8192]{2,1,0:T(8,128)(2,1)}, u32[]{:S(2)}, u32[]{:S(2)}) collective-permute-start(bf16[2,24,8192]{2,1,0:T(8,128)(2,1)} %collective-permute-done.5), channel_id=1, source_target_pairs={{0,1},{1,2},{2,3},{3,4},{4,5},{5,6},{6,7},{7,0},{8,9},{9,10},{10,1... | collective-permute-start | bytes 2359304 | tf_op jit(solution)/shard_map/ppermute | solution.py:16
  165.2 11.4 %copy-start.2 = (bf16[2,24,8192]{2,1,0:T(8,128)(2,1)S(1)}, bf16[2,24,8192]{2,1,0:T(8,128)(2,1)}, u32[]{:S(2)}) copy-start(bf16[2,24,8192]{2,1,0:T(8,128)(2,1)} %param.8) | copy-start | bytes 2359300
  165.2 308.7 %all-reduce.8.cloned.1.call-start = ((), (), s32[]{:S(2)}) async-start(), calls=%async_computation.2 | async-start | bytes 6291456 | tf_op jit(solution)/shard_map/psum | solution.py:24
  165.2 8.5 %copy-start.4 = (bf16[2,24,8192]{2,1,0:T(8,128)(2,1)S(1)}, bf16[2,24,8192]{2,1,0:T(8,128)(2,1)}, u32[]{:S(2)}) copy-start(bf16[2,24,8192]{2,1,0:T(8,128)(2,1)} %copy-done.3) | copy-start | bytes 2359300
  408.9 310.8 %all-reduce.10.cloned.1.call-start = ((), (), s32[]{:S(2)}) async-start(), calls=%async_computation.3 | async-start | bytes 12582912 | tf_op jit(solution)/shard_map/psum | solution.py:50
  508.2 2.2 copy-start.5
  747.7 10.3 %copy-start.1 = (bf16[96,4096]{1,0:T(8,128)(2,1)S(1)}, bf16[96,4096]{1,0:T(8,128)(2,1)}, u32[]{:S(2)}) copy-start(bf16[96,4096]{1,0:T(8,128)(2,1)} %param.6) | copy-start | bytes 2359300
Sparse Core Ops, SparseCore 0:
  10.4 30.4 all-gather.1
  165.3 211.7 all-reduce.5
  409.1 64.7 all-reduce.7
  508.4 211.3 all-reduce.9
